TPU v7x, 128 devices: a whole 4x4x4 slice. The times are simulated.
128 devices in a mesh: lon: 32 (over z, y, core), lat: 4 (over x).
Axes of the slice: x: 4, y: 4, z: 4, core: 2. Of those that a mesh axis runs over, the one named last changes fastest.
Arguments:
- state: float32 [32, 2048, 6, 128], P('lat', 'lon'), may hold values from -4 to 4
- background: float32 [32, 2048, 6, 128], P('lat', 'lon'), may hold values from -4 to 4
- diffusivity: float32 [32, 2048, 128], P('lat', 'lon'), may hold values from 0.03 to 0.2
- radiances: bfloat16 [2, 32, 2048, 512], P(None, 'lat', 'lon'), may hold values from -5 to 5
- owners: int32 [2, 4, 512], P(None, 'lat', 'lon'), may hold values from 0 to 31, as said below
- first_layer: bfloat16 [32, 768, 1024], P('lon'), may hold values from -0.21875 to 0.21875
- second_layer: bfloat16 [32, 1024, 1024], P('lon'), may hold values from -0.1875 to 0.1875
- third_layer: bfloat16 [32, 1024, 512], P('lon'), may hold values from -0.1875 to 0.1875
- channel_weight: float32 [32, 512], P('lon'), may hold values from 0.3 to 3
Outputs:
- gradient: float32 [32, 2048, 6, 128], P('lat', 'lon')
Inputs may be any that keep to these rules, and one draw needn't show every extreme that they name: `owners`: every block is observed by one instrument in every slot. In each slot a device sends at most 1 of its blocks to one instrument, and an instrument receives at most 24 blocks from the devices of one latitude index; both bounds are reached in every slot and latitude index.
All inputs are finite; a program needn't handle non-finite values.
Results may differ from a plain program's by a relative error of at most 0.0024.
Values may be sent and summed in bfloat16 or wider, within the bound.
A program may use at most 128 MiB of HBM per device.

v0:
```python
import functools

import jax
import jax.numpy as jnp
from jax import lax
from jax.experimental import pallas as pl
from jax.experimental.pallas import tpu as pltpu
from jax.sharding import PartitionSpec as P

MESH = pl.DeviceIdType.MESH
F32 = jnp.float32
BF16 = jnp.bfloat16
ADVECT = 0.125
VERTICAL = 0.1
BLK = 32
CHUNK = 8
TILE = 256
PAD = 8


def torus(n_lon):
    chips = n_lon // 2
    ny = 1
    while ny * ny < chips:
        ny *= 2
    return chips // ny, ny


def offset_order(n_lon):
    nz, ny = torus(n_lon)

    def hops(d):
        return min(d[0], nz - d[0]) + min(d[1], ny - d[1])

    chips = []
    for d in sorted(((a, b) for a in range(nz) for b in range(ny) if a or b), key=lambda d: (hops(d), d)):
        opposite = ((nz - d[0]) % nz, (ny - d[1]) % ny)
        for e in (d, opposite):
            if e not in chips:
                chips.append(e)
    return [(0, 0, 0), (0, 0, 1)] + [(a, b, c) for c in (0, 1) for a, b in chips]


def kernel(
    n_lon, n_lat, pick, slotk,
    st, bg, kd, rad, w1h, w2h, w3h, cwh,
    out,
    s0, s1, kap, rst, cols, send_r, send_c, recv_r, recv_c, rep_s, rep_0, rep_1,
    w1, w2, w3, cw, bgv, frc, acc, north, south, flux, edge_s, edge_r,
    a1, g1, a2, g2, mis, gg2, gg1,
    load_sem, out_sem, cs_sem, cr_sem, rs_sem, rr_sem, ps_sem, pr_sem,
    ns_s, ns_r, ew_s, ew_r,
):
    rows, fields, width, levels = st.shape
    halves = width // BLK
    nz, ny = torus(n_lon)
    order = offset_order(n_lon)
    chunk = min(CHUNK, n_lon // 4)
    chunks = n_lon // chunk
    lon = lax.axis_index("lon")
    lat = lax.axis_index("lat")
    core = lax.rem(lon, 2)
    yy = lax.rem(lon // 2, ny)
    zz = lon // (2 * ny)
    z_at = [lax.rem(zz + d, nz) * (2 * ny) for d in range(nz)]
    y_at = [lax.rem(yy + d, ny) * 2 for d in range(ny)]
    c_at = [core, 1 - core]

    rep_r = (rep_0, rep_1)

    def to(k):
        a, b, c = order[k]
        return (z_at[a] + y_at[b] + c_at[c], lat)

    def back(k):
        a, b, c = order[k]
        return (z_at[(nz - a) % nz] + y_at[(ny - b) % ny] + c_at[c], lat)

    up = (lon, lax.rem(lat + 1, n_lat))
    down = (lon, lax.rem(lat + n_lat - 1, n_lat))
    east = (lax.rem(lon + 1, n_lon), lat)
    west = (lax.rem(lon + n_lon - 1, n_lon), lat)
    inner = pl.ds(PAD, width)

    loads = [
        (st, s0.at[pl.ds(1, rows), :, inner, :]),
        (kd, kap), (rad, rst), (w1h, w1), (w2h, w2), (w3h, w3), (cwh, cw), (bg, bgv),
    ]
    loads = [pltpu.make_async_copy(src, dst, load_sem.at[i]) for i, (src, dst) in enumerate(loads)]
    for load in loads:
        load.start()

    barrier = pltpu.get_barrier_semaphore()
    for k in range(1, n_lon):
        pl.semaphore_signal(barrier, inc=1, device_id=to(k), device_id_type=MESH)
    for there in (up, down):
        pl.semaphore_signal(barrier, inc=1, device_id=there, device_id_type=MESH)
    pl.semaphore_wait(barrier, n_lon + 1)

    def remote(src, dst, send_sem, recv_sem, there):
        return pltpu.make_async_remote_copy(
            src_ref=src, dst_ref=dst, send_sem=send_sem, recv_sem=recv_sem,
            device_id=there, device_id_type=MESH,
        )

    def send_rows(phase, row_up, to_up, row_down, to_down):
        remote(row_up, to_up, ns_s.at[phase, 0], ns_r.at[phase, 0], up).start()
        remote(row_down, to_down, ns_s.at[phase, 1], ns_r.at[phase, 1], down).start()

    def send_edges(phase):
        for side, there in ((0, east), (1, west)):
            remote(
                edge_s.at[phase, side], edge_r.at[phase, side],
                ew_s.at[phase, side], ew_r.at[phase, side], there,
            ).start()

    def wait_halo(phase, row_up, to_up, row_down, to_down):
        remote(row_up, to_up, ns_s.at[phase, 0], ns_r.at[phase, 0], up).wait()
        remote(row_down, to_down, ns_s.at[phase, 1], ns_r.at[phase, 1], down).wait()
        for side, there in ((0, east), (1, west)):
            remote(
                edge_s.at[phase, side], edge_r.at[phase, side],
                ew_s.at[phase, side], ew_r.at[phase, side], there,
            ).wait()

    def state_rows(s):
        return (
            s.at[rows, :, inner, :], s.at[0, :, inner, :],
            s.at[1, :, inner, :], s.at[rows + 1, :, inner, :],
        )

    def send_state(phase, s):
        send_rows(phase, *state_rows(s))

        @pl.loop(0, rows)
        def _(i):
            for f in range(fields):
                edge_s[phase, 0, i, f : f + 1, :] = s[i + 1, f, PAD + width - 1 : PAD + width, :]
                edge_s[phase, 1, i, f : f + 1, :] = s[i + 1, f, PAD : PAD + 1, :]

        send_edges(phase)

    def take_state(phase, s):
        wait_halo(phase, *state_rows(s))

        @pl.loop(0, rows)
        def _(i):
            for f in range(fields):
                s[i + 1, f, PAD - 1 : PAD, :] = edge_r[phase, 0, i, f : f + 1, :]
                s[i + 1, f, PAD + width : PAD + width + 1, :] = edge_r[phase, 1, i, f : f + 1, :]

        @pl.when(lat == 0)
        def _():
            s[0, :, PAD : PAD + width, :] = jnp.zeros((fields, width, levels), F32)

        @pl.when(lat == n_lat - 1)
        def _():
            s[rows + 1, :, PAD : PAD + width, :] = jnp.zeros((fields, width, levels), F32)

    level = lax.broadcasted_iota(jnp.int32, (BLK, levels), 1)
    from_below = jnp.where(level == 0, 0.0, VERTICAL).astype(F32)
    from_above = jnp.where(level == levels - 1, 0.0, VERTICAL).astype(F32)

    def vertical(v):
        return from_below * pltpu.roll(v, 1, 1) + from_above * pltpu.roll(v, levels - 1, 1)

    def advance(s, slot, keep):
        @pl.loop(0, rows)
        def _(i):
            for h in range(halves):
                at = PAD + h * BLK
                k = kap[i, h * BLK : (h + 1) * BLK, :]
                u = ADVECT * s[i + 1, 0, at : at + BLK, :]
                v = ADVECT * s[i + 1, 1, at : at + BLK, :]
                k_e, k_w, k_n, k_s = k - u, k + u, k - v, k + v
                k_c = (1.0 - 2.0 * VERTICAL) - 4.0 * k
                for f in range(fields):
                    c = s[i + 1, f, at : at + BLK, :]
                    new = (
                        k_c * c
                        + k_e * s[i + 1, f, at + 1 : at + 1 + BLK, :]
                        + k_w * s[i + 1, f, at - 1 : at - 1 + BLK, :]
                        + k_n * s[i + 2, f, at : at + BLK, :]
                        + k_s * s[i, f, at : at + BLK, :]
                        + vertical(c)
                    )
                    if keep is not None:
                        keep[i + 1, f, at : at + BLK, :] = new
                    cols[slot, i * halves + h, :, f * levels : (f + 1) * levels] = new.astype(BF16)

    def dispatch(slot, blocks, sent, got, send_sem, recv_sem):
        got[slot, 0] = blocks[slot, pick[slot, 0]]
        for k in range(1, n_lon):
            sent[slot, k] = blocks[slot, pick[slot, k]]
            remote(
                sent.at[slot, k], got.at[slot, k], send_sem.at[slot],
                recv_sem.at[slot, k // chunk], to(k),
            ).start()

    loads[0].wait()
    send_state(0, s0)
    loads[2].wait()
    dispatch(1, rst, send_r, recv_r, rs_sem, rr_sem)
    loads[1].wait()
    take_state(0, s0)
    advance(s0, 0, s1)
    send_state(1, s1)
    dispatch(0, rst, send_r, recv_r, rs_sem, rr_sem)
    take_state(1, s1)
    advance(s1, 1, None)
    dispatch(1, cols, send_c, recv_c, cs_sem, cr_sem)
    dispatch(0, cols, send_c, recv_c, cs_sem, cr_sem)
    for load in loads[3:]:
        load.wait()

    span = chunk * BLK
    h1, h2, ch, cin = w1.shape[1], w2.shape[1], w3.shape[1], w1.shape[0]

    def tiles(n):
        return [slice(a, min(a + TILE, n)) for a in range(0, n, TILE)]

    def nn(a, b):
        return lax.dot_general(a, b, (((1,), (0,)), ((), ())), preferred_element_type=F32)

    def nt(a, b):
        return lax.dot_general(a, b, (((1,), (1,)), ((), ())), preferred_element_type=F32)

    def activate(z):
        sig = 0.5 * jnp.tanh(0.5 * z) + 0.5
        act = z * sig
        return act.astype(BF16), sig + act * (1.0 - sig)

    def wait_chunk(got, sem, slot, g):
        for first in (True, False):
            @pl.when((g == 0) if first else (g > 0))
            def _():
                part = got.at[slot, pl.ds(1, chunk - 1)] if first else got.at[slot, pl.ds(g * chunk, chunk)]
                pltpu.make_async_copy(part, part, sem.at[slot, g]).wait()

    @pl.loop(0, 2 * chunks)
    def _(t):
        slot = 1 - t // chunks
        g = lax.rem(t, chunks)
        base = g * chunk
        wait_chunk(recv_r, rr_sem, slot, g)
        wait_chunk(recv_c, cr_sem, slot, g)
        for n in tiles(h1):
            x = recv_c[slot, pl.ds(base, chunk)].reshape(span, cin)
            a1[:, n], g1[:, n] = activate(nn(x, w1[:, n]))
        for n in tiles(h2):
            a2[:, n], g2[:, n] = activate(nn(a1[...], w2[:, n]))
        for n in tiles(ch):
            y = recv_r[slot, pl.ds(base, chunk), :, n].reshape(span, n.stop - n.start).astype(F32)
            mis[:, n] = (cw[:, n] * (nn(a2[...], w3[:, n]) - y)).astype(BF16)
        for n in tiles(h2):
            gg2[:, n] = (nt(mis[...], w3[n, :]) * g2[:, n]).astype(BF16)
        for n in tiles(h1):
            gg1[:, n] = (nt(gg2[...], w2[n, :]) * g1[:, n]).astype(BF16)
        for n in tiles(cin):
            rep_s[slot, pl.ds(base, chunk), :, n] = (
                nt(gg1[...], w1[n, :]).astype(BF16).reshape(chunk, BLK, n.stop - n.start)
            )
        for tt in range(2 * chunks):
            @pl.when(t == tt)
            def _():
                home, replies = 1 - tt // chunks, rep_r[1 - tt // chunks]
                for k in range(tt % chunks * chunk, (tt % chunks + 1) * chunk):
                    if k == 0:
                        replies[0] = rep_s[home, 0]
                    else:
                        remote(
                            rep_s.at[home, k], replies.at[k], ps_sem.at[home],
                            pr_sem.at[home], back(k),
                        ).start()


    def wait_replies(slot):
        part = rep_r[slot].at[pl.ds(1, n_lon - 1)]
        pltpu.make_async_copy(part, part, pr_sem.at[slot]).wait()

    def unpack(slot):
        @pl.loop(0, rows)
        def _(i):
            for h in range(halves):
                k = slotk[slot, i * halves + h]
                for f in range(fields):
                    frc[i, f, h * BLK : (h + 1) * BLK, :] = rep_r[slot][
                        k, :, f * levels : (f + 1) * levels
                    ].astype(F32)

    def flux_rows(phase, s, i):
        for h in range(halves):
            part = slice(h * BLK, (h + 1) * BLK)
            k = kap[i, part, :]
            v = ADVECT * s[i + 1, 1, PAD + h * BLK : PAD + (h + 1) * BLK, :]
            k_n, k_s = k - v, k + v
            for f in range(fields):
                g = frc[i, f, part, :]
                north[phase - 2, i + 1, f, part, :] = g * k_n
                south[phase - 2, i, f, part, :] = g * k_s

    def adjoint_rows(phase):
        n, s = north.at[phase - 2], south.at[phase - 2]
        return (n.at[rows], n.at[0], s.at[0], s.at[rows])

    def send_adjoint(phase, s):
        flux_rows(phase, s, 0)
        flux_rows(phase, s, rows - 1)
        send_rows(phase, *adjoint_rows(phase))

        @pl.loop(0, rows)
        def _(i):
            for side, j in ((0, width - 1), (1, 0)):
                k = kap[i, j : j + 1, :]
                u = ADVECT * s[i + 1, 0, PAD + j : PAD + j + 1, :]
                coef = k - u if side == 0 else k + u
                for f in range(fields):
                    edge_s[phase, side, i, f : f + 1, :] = coef * frc[i, f, j : j + 1, :]

        send_edges(phase)

        @pl.loop(1, rows - 1)
        def _(i):
            flux_rows(phase, s, i)

    def local_adjoint(s):
        for f in range(fields):
            flux[0, f, 0:PAD, :] = jnp.zeros((PAD, levels), F32)
            flux[1, f, PAD + width :, :] = jnp.zeros((PAD, levels), F32)

        @pl.loop(0, rows)
        def _(i):
            for h in range(halves):
                at = PAD + h * BLK
                k = kap[i, h * BLK : (h + 1) * BLK, :]
                u = ADVECT * s[i + 1, 0, at : at + BLK, :]
                k_e, k_w = k - u, k + u
                for f in range(fields):
                    g = frc[i, f, h * BLK : (h + 1) * BLK, :]
                    flux[0, f, at : at + BLK, :] = k_e * g
                    flux[1, f, at : at + BLK, :] = k_w * g
            for h in range(halves):
                part = slice(h * BLK, (h + 1) * BLK)
                at = PAD + h * BLK
                k_c = (1.0 - 2.0 * VERTICAL) - 4.0 * kap[i, part, :]
                zonal = jnp.zeros((BLK, levels), F32)
                merid = jnp.zeros((BLK, levels), F32)
                for f in reversed(range(fields)):
                    g = frc[i, f, part, :]
                    zonal += g * (s[i + 1, f, at + 1 : at + 1 + BLK, :] - s[i + 1, f, at - 1 : at - 1 + BLK, :])
                    merid += g * (s[i + 2, f, at : at + BLK, :] - s[i, f, at : at + BLK, :])
                    own = (
                        k_c * g + vertical(g)
                        + flux[0, f, at - 1 : at - 1 + BLK, :] + flux[1, f, at + 1 : at + 1 + BLK, :]
                    )
                    acc[i, f, part, :] = own
                acc[i, 0, part, :] -= ADVECT * zonal
                acc[i, 1, part, :] -= ADVECT * merid

    def finish_adjoint(phase, done):
        wait_halo(phase, *adjoint_rows(phase))

        @pl.when(lat == 0)
        def _():
            north[phase - 2, 0] = jnp.zeros((fields, width, levels), F32)

        @pl.when(lat == n_lat - 1)
        def _():
            south[phase - 2, rows] = jnp.zeros((fields, width, levels), F32)

        @pl.loop(0, rows)
        def _(i):
            for f in range(fields):
                acc[i, f, 0:1, :] += edge_r[phase, 0, i, f : f + 1, :]
                acc[i, f, width - 1 : width, :] += edge_r[phase, 1, i, f : f + 1, :]
            for h in range(halves):
                part = slice(h * BLK, (h + 1) * BLK)
                for f in range(fields):
                    total = acc[i, f, part, :] + north[phase - 2, i, f, part, :] + south[phase - 2, i + 1, f, part, :]
                    done(i, h, f, part, total)

    def to_costate(i, h, f, part, total):
        forced = rep_0[slotk[0, i * halves + h], :, f * levels : (f + 1) * levels]
        frc[i, f, part, :] = forced.astype(F32) + total

    def to_gradient(i, h, f, part, total):
        own = s0[i + 1, f, PAD + part.start : PAD + part.stop, :]
        acc[i, f, part, :] = (own - bgv[i, f, part, :]) + total
        if h == halves - 1 and f == fields - 1:
            pltpu.make_async_copy(acc.at[i], out.at[i], out_sem).start()

    wait_replies(1)
    unpack(1)
    send_adjoint(2, s1)
    local_adjoint(s1)
    wait_replies(0)
    finish_adjoint(2, to_costate)
    send_adjoint(3, s0)
    local_adjoint(s0)
    finish_adjoint(3, to_gradient)

    for slot in (0, 1):
        for buffer, sem in ((send_r, rs_sem), (send_c, cs_sem), (rep_s, ps_sem)):
            part = buffer.at[slot, pl.ds(1, n_lon - 1)]
            pltpu.make_async_copy(part, part, sem.at[slot]).wait()
    pltpu.make_async_copy(acc, out, out_sem).wait()


def shards(state, background, diffusivity, radiances, owners, first, second, third, weight):
    n_lon, n_lat = lax.axis_size("lon"), lax.axis_size("lat")
    rows, width, fields, levels = state.shape
    blocks = owners.shape[2]
    channels = radiances.shape[3]
    cin, h1, h2 = first.shape[1], first.shape[2], second.shape[2]
    nz, ny = torus(n_lon)
    order = offset_order(n_lon)
    chunk = min(CHUNK, n_lon // 4)
    span = chunk * BLK

    lon = lax.axis_index("lon")
    peers = jnp.stack(
        [
            lax.rem(lon // (2 * ny) + a, nz) * (2 * ny) + lax.rem(lax.rem(lon // 2, ny) + b, ny) * 2 + lax.rem(lon + c, 2)
            for a, b, c in order
        ]
    )
    owner = owners[:, 0, :]
    match = owner[:, None, :] == peers[None, :, None]
    pick = jnp.sum(jnp.where(match, jnp.arange(blocks, dtype=jnp.int32)[None, None, :], 0), axis=2)
    slotk = jnp.sum(jnp.where(match, jnp.arange(n_lon, dtype=jnp.int32)[None, :, None], 0), axis=1)

    smem = pl.BlockSpec(memory_space=pltpu.SMEM)
    hbm = pl.BlockSpec(memory_space=pl.ANY)
    dma = pltpu.SemaphoreType.DMA
    body = functools.partial(kernel, n_lon, n_lat)
    slots = 2
    field = (rows, fields, width, levels)
    result = pl.pallas_call(
        body,
        out_shape=jax.ShapeDtypeStruct(field, F32),
        in_specs=[smem, smem] + [hbm] * 8,
        out_specs=hbm,
        scratch_shapes=[
            pltpu.VMEM((rows + 2, fields, width + 2 * PAD, levels), F32),
            pltpu.VMEM((rows + 2, fields, width + 2 * PAD, levels), F32),
            pltpu.VMEM((rows, width, levels), F32),
            pltpu.VMEM((slots, blocks, BLK, channels), BF16),
            pltpu.VMEM((slots, blocks, BLK, cin), BF16),
            pltpu.VMEM((slots, n_lon, BLK, channels), BF16),
            pltpu.VMEM((slots, n_lon, BLK, cin), BF16),
            pltpu.VMEM((slots, n_lon, BLK, channels), BF16),
            pltpu.VMEM((slots, n_lon, BLK, cin), BF16),
            pltpu.VMEM((slots, n_lon, BLK, cin), BF16),
            pltpu.VMEM((n_lon, BLK, cin), BF16),
            pltpu.VMEM((n_lon, BLK, cin), BF16),
            pltpu.VMEM((cin, h1), BF16),
            pltpu.VMEM((h1, h2), BF16),
            pltpu.VMEM((h2, channels), BF16),
            pltpu.VMEM((1, channels), F32),
            pltpu.VMEM(field, F32),
            pltpu.VMEM(field, F32),
            pltpu.VMEM(field, F32),
            pltpu.VMEM((2, rows + 1, fields, width, levels), F32),
            pltpu.VMEM((2, rows + 1, fields, width, levels), F32),
            pltpu.VMEM((2, fields, width + 2 * PAD, levels), F32),
            pltpu.VMEM((4, 2, rows, 8, levels), F32),
            pltpu.VMEM((4, 2, rows, 8, levels), F32),
            pltpu.VMEM((span, h1), BF16),
            pltpu.VMEM((span, h1), F32),
            pltpu.VMEM((span, h2), BF16),
            pltpu.VMEM((span, h2), F32),
            pltpu.VMEM((span, channels), BF16),
            pltpu.VMEM((span, h2), BF16),
            pltpu.VMEM((span, h1), BF16),
            dma((8,)),
            dma,
            dma((slots,)),
            dma((slots, n_lon // chunk)),
            dma((slots,)),
            dma((slots, n_lon // chunk)),
            dma((slots,)),
            dma((slots,)),
            dma((4, 2)),
            dma((4, 2)),
            dma((4, 2)),
            dma((4, 2)),
        ],
        compiler_params=pltpu.CompilerParams(
            collective_id=0, has_side_effects=True, vmem_limit_bytes=56 * 2**20
        ),
        name="gradient",
    )(
        pick,
        slotk,
        state.transpose(0, 2, 1, 3),
        background.transpose(0, 2, 1, 3),
        diffusivity,
        radiances.reshape(slots, blocks, BLK, channels),
        first[0],
        second[0],
        third[0],
        weight,
    )
    return result.transpose(0, 2, 1, 3)


def solution(mesh):
    placed = (
        P("lat", "lon", None, None),
        P("lat", "lon", None, None),
        P("lat", "lon", None),
        P(None, "lat", "lon", None),
        P(None, "lat", "lon"),
        P("lon", None, None),
        P("lon", None, None),
        P("lon", None, None),
        P("lon", None),
    )
    return jax.shard_map(
        shards, mesh=mesh, in_specs=placed, out_specs=P("lat", "lon", None, None), check_vma=False
    )
```

profile of v0, /device:TPU:0, one launch (start us, length us, event | category | flops | bytes accessed | tf_op | source)
XLA Modules:
  0.0 116.1 jit_solution(14365713827932825929)
XLA Ops:
  0.0 0.1 stack.131
  0.1 1.4 %fusion.1 = (s32[2,16]{1,0:T(2,128)}, s32[2,32]{1,0:T(2,128)}) fusion(s32[32]{0:T(128)S(1)} %stack.131, s32[2,16]{1,0:T(2,128)} %bitcast.47), kind=kLoop, calls=%fused_computation.3 | loop fusion | flops 5024 | bytes 640 | tf_op jit(solution)/shard_map/reduce_sum | solution.py:430
  1.6 111.8 %gradient.1 = f32[8,6,64,128]{3,2,1,0:T(8,128)} custom-call(s32[2,32]{1,0:T(2,128)} %get-tuple-element.6.pick, s32[2,16]{1,0:T(2,128)} %get-tuple-element.5.slotk, f32[8,6,64,128]{3,2,1,0:T(8,128)} %bitcast.42, f32[8,6,64,128]{3,2,1,0:T(8,128)} %bitcast.43, f32[8,64,128]{2,1,0:T(8,128)} %kd.1, bf16[2,16,32,512]{3,2,1,0:T(8,128)(2,1)} %bitcast.45, ...), custom_call_target="tpu_custom_call" | custom-call | tf_op jit(solution)/shard_map/gradient/pallas_call | solution.py:438
  113.4 2.7 %copy.11 = f32[8,64,6,128]{3,1,2,0:T(8,128)} copy(f32[8,64,6,128]{3,1,2,0:T(8,128)} %bitcast.40) | data formatting | bytes 3145728
where the time goes:
time: 116 us
  Pallas kernels  112 us (97%)
  local copies, waits for them, and re-layouts  2.84 us (2%)
  other arithmetic  1.44 us (1%)
    pallas_call x1, Pallas kernels, shards(): pl.pallas_call(body, out_shape=jax.ShapeDtypeStruct(field, F32), in_specs...  112 us
    unnamed x1, local copies, waits for them, and re-layouts  2.73 us

commit v1 on v0

--- a/solution.py
+++ b/solution.py
@@ -42,13 +42,13 @@
 
 
 def kernel(
-    n_lon, n_lat, pick, slotk,
+    n_lon, n_lat, own_h,
     st, bg, kd, rad, w1h, w2h, w3h, cwh,
-    out,
+    acc,
     s0, s1, kap, rst, cols, send_r, send_c, recv_r, recv_c, rep_s, rep_0, rep_1,
-    w1, w2, w3, cw, bgv, frc, acc, north, south, flux, edge_s, edge_r,
+    w1, w2, w3, cw, bgv, frc_a, frc_b, rim_s, rim_r, flux, edge_s, edge_r, own, pick, slotk, place,
     a1, g1, a2, g2, mis, gg2, gg1,
-    load_sem, out_sem, cs_sem, cr_sem, rs_sem, rr_sem, ps_sem, pr_sem,
+    load_sem, cs_sem, cr_sem, rs_sem, rr_sem, ps_sem, pr_sem,
     ns_s, ns_r, ew_s, ew_r,
 ):
     rows, fields, width, levels = st.shape
@@ -83,11 +83,11 @@
     inner = pl.ds(PAD, width)
 
     loads = [
-        (st, s0.at[pl.ds(1, rows), :, inner, :]),
-        (kd, kap), (rad, rst), (w1h, w1), (w2h, w2), (w3h, w3), (cwh, cw), (bg, bgv),
+        (st, s0.at[pl.ds(1, rows), :, inner, :]), (rad.at[1], rst.at[1]), (kd, kap.at[pl.ds(1, rows)]),
+        (rad.at[0], rst.at[0]), (own_h, own), (w1h, w1), (w2h, w2), (w3h, w3), (cwh, cw), (bg, bgv),
     ]
     loads = [pltpu.make_async_copy(src, dst, load_sem.at[i]) for i, (src, dst) in enumerate(loads)]
-    for load in loads:
+    for load in loads[:5]:
         load.start()
 
     barrier = pltpu.get_barrier_semaphore()
@@ -95,7 +95,28 @@
         pl.semaphore_signal(barrier, inc=1, device_id=to(k), device_id_type=MESH)
     for there in (up, down):
         pl.semaphore_signal(barrier, inc=1, device_id=there, device_id_type=MESH)
-    pl.semaphore_wait(barrier, n_lon + 1)
+    for load in loads[5:]:
+        load.start()
+
+    for k, (a, b, c) in enumerate(order):
+        place[(a * ny + b) * 2 + c] = k
+
+    def find_blocks(slot):
+        found = []
+        for b in range(own.shape[2]):
+            owner = own[slot, 0, b]
+            a = lax.rem(owner // (2 * ny) - zz + nz, nz)
+            d = lax.rem(lax.rem(owner // 2, ny) - yy + ny, ny)
+            c = lax.rem(lax.rem(owner, 2) + core, 2)
+            found.append(place[(a * ny + d) * 2 + c])
+            slotk[slot, b] = found[-1]
+
+        @pl.loop(0, n_lon)
+        def _(k):
+            block = jnp.int32(0)
+            for b, at in enumerate(found):
+                block = jnp.where(at == k, b, block)
+            pick[slot, k] = block
 
     def remote(src, dst, send_sem, recv_sem, there):
         return pltpu.make_async_remote_copy(
@@ -114,9 +135,11 @@
                 ew_s.at[phase, side], ew_r.at[phase, side], there,
             ).start()
 
-    def wait_halo(phase, row_up, to_up, row_down, to_down):
+    def wait_rows(phase, row_up, to_up, row_down, to_down):
         remote(row_up, to_up, ns_s.at[phase, 0], ns_r.at[phase, 0], up).wait()
         remote(row_down, to_down, ns_s.at[phase, 1], ns_r.at[phase, 1], down).wait()
+
+    def wait_edges(phase):
         for side, there in ((0, east), (1, west)):
             remote(
                 edge_s.at[phase, side], edge_r.at[phase, side],
@@ -129,19 +152,20 @@
             s.at[1, :, inner, :], s.at[rows + 1, :, inner, :],
         )
 
-    def send_state(phase, s):
-        send_rows(phase, *state_rows(s))
-
+    def pack_state(phase, s):
         @pl.loop(0, rows)
         def _(i):
             for f in range(fields):
                 edge_s[phase, 0, i, f : f + 1, :] = s[i + 1, f, PAD + width - 1 : PAD + width, :]
                 edge_s[phase, 1, i, f : f + 1, :] = s[i + 1, f, PAD : PAD + 1, :]
 
+    def send_state(phase, s):
+        send_rows(phase, *state_rows(s))
         send_edges(phase)
 
     def take_state(phase, s):
-        wait_halo(phase, *state_rows(s))
+        wait_rows(phase, *state_rows(s))
+        wait_edges(phase)
 
         @pl.loop(0, rows)
         def _(i):
@@ -169,7 +193,7 @@
         def _(i):
             for h in range(halves):
                 at = PAD + h * BLK
-                k = kap[i, h * BLK : (h + 1) * BLK, :]
+                k = kap[i + 1, h * BLK : (h + 1) * BLK, :]
                 u = ADVECT * s[i + 1, 0, at : at + BLK, :]
                 v = ADVECT * s[i + 1, 1, at : at + BLK, :]
                 k_e, k_w, k_n, k_s = k - u, k + u, k - v, k + v
@@ -188,30 +212,61 @@
                         keep[i + 1, f, at : at + BLK, :] = new
                     cols[slot, i * halves + h, :, f * levels : (f + 1) * levels] = new.astype(BF16)
 
-    def dispatch(slot, blocks, sent, got, send_sem, recv_sem):
+    def pack(slot, blocks, sent, got):
         got[slot, 0] = blocks[slot, pick[slot, 0]]
         for k in range(1, n_lon):
             sent[slot, k] = blocks[slot, pick[slot, k]]
+
+    def dispatch(slot, sent, got, send_sem, recv_sem):
+        for k in range(1, n_lon):
             remote(
                 sent.at[slot, k], got.at[slot, k], send_sem.at[slot],
                 recv_sem.at[slot, k // chunk], to(k),
             ).start()
 
+    def send_columns(slot):
+        recv_c[slot, 0] = cols[slot, pick[slot, 0]]
+        for k in range(1, n_lon):
+            send_c[slot, k] = cols[slot, pick[slot, k]]
+            remote(
+                send_c.at[slot, k], recv_c.at[slot, k], cs_sem.at[slot],
+                cr_sem.at[slot, k // chunk], to(k),
+            ).start()
+
+    loads[4].wait()
+    find_blocks(1)
     loads[0].wait()
+    pack_state(0, s0)
+    loads[1].wait()
+    loads[3].wait()
+    pack(1, rst, send_r, recv_r)
+    pl.semaphore_wait(barrier, n_lon + 1)
     send_state(0, s0)
+    dispatch(1, send_r, recv_r, rs_sem, rr_sem)
+    find_blocks(0)
+    pack(0, rst, send_r, recv_r)
+    dispatch(0, send_r, recv_r, rs_sem, rr_sem)
     loads[2].wait()
-    dispatch(1, rst, send_r, recv_r, rs_sem, rr_sem)
-    loads[1].wait()
     take_state(0, s0)
     advance(s0, 0, s1)
+    pack_state(1, s1)
     send_state(1, s1)
-    dispatch(0, rst, send_r, recv_r, rs_sem, rr_sem)
     take_state(1, s1)
     advance(s1, 1, None)
-    dispatch(1, cols, send_c, recv_c, cs_sem, cr_sem)
-    dispatch(0, cols, send_c, recv_c, cs_sem, cr_sem)
-    for load in loads[3:]:
+    send_columns(1)
+    send_columns(0)
+    for load in loads[5:]:
         load.wait()
+
+    @pl.loop(0, rows)
+    def _(i):
+        for f in range(fields):
+            bgv[i, f] = s0[i + 1, f, PAD : PAD + width, :] - bgv[i, f]
+
+    for i in (0, rows + 1):
+        kap[i] = jnp.zeros((width, levels), F32)
+        frc_a[i] = jnp.zeros((fields, width, levels), F32)
+        frc_b[i] = jnp.zeros((fields, width, levels), F32)
 
     span = chunk * BLK
     h1, h2, ch, cin = w1.shape[1], w2.shape[1], w3.shape[1], w1.shape[0]
@@ -278,132 +333,124 @@
         part = rep_r[slot].at[pl.ds(1, n_lon - 1)]
         pltpu.make_async_copy(part, part, pr_sem.at[slot]).wait()
 
-    def unpack(slot):
+    def forced(slot, i, h, f):
+        return rep_r[slot][slotk[slot, i * halves + h], :, f * levels : (f + 1) * levels].astype(F32)
+
+    def rims(phase):
+        out_rim, in_rim = rim_s.at[phase - 2], rim_r.at[phase - 2]
+        return (out_rim.at[0], in_rim.at[0], out_rim.at[1], in_rim.at[1])
+
+    def send_rims(phase, s, g):
+        for side, i, sign in ((0, rows, -1.0), (1, 1, 1.0)):
+            for h in range(halves):
+                part = slice(h * BLK, (h + 1) * BLK)
+                coef = kap[i, part, :] + (sign * ADVECT) * s[i, 1, PAD + h * BLK : PAD + (h + 1) * BLK, :]
+                for f in range(fields):
+                    rim_s[phase - 2, side, f, part, :] = (coef * g[i, f, part, :]).astype(BF16)
+        send_rows(phase, *rims(phase))
+
+    def send_sides(phase, s, g):
         @pl.loop(0, rows)
         def _(i):
-            for h in range(halves):
-                k = slotk[slot, i * halves + h]
+            for side, j, sign in ((0, width - 1, -1.0), (1, 0, 1.0)):
+                coef = kap[i + 1, j : j + 1, :] + (sign * ADVECT) * s[i + 1, 0, PAD + j : PAD + j + 1, :]
                 for f in range(fields):
-                    frc[i, f, h * BLK : (h + 1) * BLK, :] = rep_r[slot][
-                        k, :, f * levels : (f + 1) * levels
-                    ].astype(F32)
-
-    def flux_rows(phase, s, i):
-        for h in range(halves):
-            part = slice(h * BLK, (h + 1) * BLK)
-            k = kap[i, part, :]
-            v = ADVECT * s[i + 1, 1, PAD + h * BLK : PAD + (h + 1) * BLK, :]
-            k_n, k_s = k - v, k + v
-            for f in range(fields):
-                g = frc[i, f, part, :]
-                north[phase - 2, i + 1, f, part, :] = g * k_n
-                south[phase - 2, i, f, part, :] = g * k_s
-
-    def adjoint_rows(phase):
-        n, s = north.at[phase - 2], south.at[phase - 2]
-        return (n.at[rows], n.at[0], s.at[0], s.at[rows])
-
-    def send_adjoint(phase, s):
-        flux_rows(phase, s, 0)
-        flux_rows(phase, s, rows - 1)
-        send_rows(phase, *adjoint_rows(phase))
-
-        @pl.loop(0, rows)
-        def _(i):
-            for side, j in ((0, width - 1), (1, 0)):
-                k = kap[i, j : j + 1, :]
-                u = ADVECT * s[i + 1, 0, PAD + j : PAD + j + 1, :]
-                coef = k - u if side == 0 else k + u
-                for f in range(fields):
-                    edge_s[phase, side, i, f : f + 1, :] = coef * frc[i, f, j : j + 1, :]
+                    edge_s[phase, side, i, f : f + 1, :] = coef * g[i + 1, f, j : j + 1, :]
 
         send_edges(phase)
 
-        @pl.loop(1, rows - 1)
-        def _(i):
-            flux_rows(phase, s, i)
-
-    def local_adjoint(s):
-        for f in range(fields):
-            flux[0, f, 0:PAD, :] = jnp.zeros((PAD, levels), F32)
-            flux[1, f, PAD + width :, :] = jnp.zeros((PAD, levels), F32)
-
+    for f in range(fields):
+        flux[0, f, 0:PAD, :] = jnp.zeros((PAD, levels), F32)
+        flux[1, f, PAD + width :, :] = jnp.zeros((PAD, levels), F32)
+
+    def transpose_tile(s, g, into, shift, extra):
         @pl.loop(0, rows)
         def _(i):
             for h in range(halves):
                 at = PAD + h * BLK
-                k = kap[i, h * BLK : (h + 1) * BLK, :]
+                k = kap[i + 1, h * BLK : (h + 1) * BLK, :]
                 u = ADVECT * s[i + 1, 0, at : at + BLK, :]
                 k_e, k_w = k - u, k + u
                 for f in range(fields):
-                    g = frc[i, f, h * BLK : (h + 1) * BLK, :]
-                    flux[0, f, at : at + BLK, :] = k_e * g
-                    flux[1, f, at : at + BLK, :] = k_w * g
+                    own_g = g[i + 1, f, h * BLK : (h + 1) * BLK, :]
+                    flux[0, f, at : at + BLK, :] = k_e * own_g
+                    flux[1, f, at : at + BLK, :] = k_w * own_g
             for h in range(halves):
                 part = slice(h * BLK, (h + 1) * BLK)
                 at = PAD + h * BLK
-                k_c = (1.0 - 2.0 * VERTICAL) - 4.0 * kap[i, part, :]
+                k_c = (1.0 - 2.0 * VERTICAL) - 4.0 * kap[i + 1, part, :]
+                k_n = kap[i, part, :] - ADVECT * s[i, 1, at : at + BLK, :]
+                k_s = kap[i + 2, part, :] + ADVECT * s[i + 2, 1, at : at + BLK, :]
                 zonal = jnp.zeros((BLK, levels), F32)
                 merid = jnp.zeros((BLK, levels), F32)
                 for f in reversed(range(fields)):
-                    g = frc[i, f, part, :]
-                    zonal += g * (s[i + 1, f, at + 1 : at + 1 + BLK, :] - s[i + 1, f, at - 1 : at - 1 + BLK, :])
-                    merid += g * (s[i + 2, f, at : at + BLK, :] - s[i, f, at : at + BLK, :])
-                    own = (
-                        k_c * g + vertical(g)
+                    own_g = g[i + 1, f, part, :]
+                    zonal += own_g * (
+                        s[i + 1, f, at + 1 : at + 1 + BLK, :] - s[i + 1, f, at - 1 : at - 1 + BLK, :]
+                    )
+                    merid += own_g * (s[i + 2, f, at : at + BLK, :] - s[i, f, at : at + BLK, :])
+                    total = (
+                        k_c * own_g + vertical(own_g)
+                        + k_n * g[i, f, part, :] + k_s * g[i + 2, f, part, :]
                         + flux[0, f, at - 1 : at - 1 + BLK, :] + flux[1, f, at + 1 : at + 1 + BLK, :]
                     )
-                    acc[i, f, part, :] = own
-                acc[i, 0, part, :] -= ADVECT * zonal
-                acc[i, 1, part, :] -= ADVECT * merid
-
-    def finish_adjoint(phase, done):
-        wait_halo(phase, *adjoint_rows(phase))
-
-        @pl.when(lat == 0)
-        def _():
-            north[phase - 2, 0] = jnp.zeros((fields, width, levels), F32)
-
-        @pl.when(lat == n_lat - 1)
-        def _():
-            south[phase - 2, rows] = jnp.zeros((fields, width, levels), F32)
+                    if extra is not None:
+                        total += extra[i, f, part, :]
+                    if f == 0:
+                        total -= ADVECT * zonal
+                    into[i + shift, f, part, :] = total
+                into[i + shift, 1, part, :] -= ADVECT * merid
+
+    def add_sides(phase, into, shift):
+        wait_edges(phase)
 
         @pl.loop(0, rows)
         def _(i):
             for f in range(fields):
-                acc[i, f, 0:1, :] += edge_r[phase, 0, i, f : f + 1, :]
-                acc[i, f, width - 1 : width, :] += edge_r[phase, 1, i, f : f + 1, :]
-            for h in range(halves):
-                part = slice(h * BLK, (h + 1) * BLK)
+                into[i + shift, f, 0:1, :] += edge_r[phase, 0, i, f : f + 1, :]
+                into[i + shift, f, width - 1 : width, :] += edge_r[phase, 1, i, f : f + 1, :]
+
+    def add_rims(phase, into, shift):
+        wait_rows(phase, *rims(phase))
+        for side, i, there in ((0, 0, lat > 0), (1, rows - 1, lat < n_lat - 1)):
+            @pl.when(there)
+            def _():
                 for f in range(fields):
-                    total = acc[i, f, part, :] + north[phase - 2, i, f, part, :] + south[phase - 2, i + 1, f, part, :]
-                    done(i, h, f, part, total)
-
-    def to_costate(i, h, f, part, total):
-        forced = rep_0[slotk[0, i * halves + h], :, f * levels : (f + 1) * levels]
-        frc[i, f, part, :] = forced.astype(F32) + total
-
-    def to_gradient(i, h, f, part, total):
-        own = s0[i + 1, f, PAD + part.start : PAD + part.stop, :]
-        acc[i, f, part, :] = (own - bgv[i, f, part, :]) + total
-        if h == halves - 1 and f == fields - 1:
-            pltpu.make_async_copy(acc.at[i], out.at[i], out_sem).start()
+                    into[i + shift, f] += rim_r[phase - 2, side, f].astype(F32)
+
+    def add_forced(i):
+        for h in range(halves):
+            for f in range(fields):
+                frc_b[i + 1, f, h * BLK : (h + 1) * BLK, :] += forced(0, i, h, f)
 
     wait_replies(1)
-    unpack(1)
-    send_adjoint(2, s1)
-    local_adjoint(s1)
+
+    @pl.loop(0, rows)
+    def _(i):
+        for h in range(halves):
+            for f in range(fields):
+                frc_a[i + 1, f, h * BLK : (h + 1) * BLK, :] = forced(1, i, h, f)
+
+    send_rims(2, s1, frc_a)
+    send_sides(2, s1, frc_a)
+    transpose_tile(s1, frc_a, frc_b, 1, None)
+    add_sides(2, frc_b, 1)
+    add_rims(2, frc_b, 1)
+
     wait_replies(0)
-    finish_adjoint(2, to_costate)
-    send_adjoint(3, s0)
-    local_adjoint(s0)
-    finish_adjoint(3, to_gradient)
+    add_forced(0)
+    add_forced(rows - 1)
+    send_rims(3, s0, frc_b)
+    pl.loop(1, rows - 1)(add_forced)
+    send_sides(3, s0, frc_b)
+    transpose_tile(s0, frc_b, acc, 0, bgv)
+    add_sides(3, acc, 0)
+    add_rims(3, acc, 0)
 
     for slot in (0, 1):
         for buffer, sem in ((send_r, rs_sem), (send_c, cs_sem), (rep_s, ps_sem)):
             part = buffer.at[slot, pl.ds(1, n_lon - 1)]
             pltpu.make_async_copy(part, part, sem.at[slot]).wait()
-    pltpu.make_async_copy(acc, out, out_sem).wait()
 
 
 def shards(state, background, diffusivity, radiances, owners, first, second, third, weight):
@@ -412,38 +459,23 @@
     blocks = owners.shape[2]
     channels = radiances.shape[3]
     cin, h1, h2 = first.shape[1], first.shape[2], second.shape[2]
-    nz, ny = torus(n_lon)
-    order = offset_order(n_lon)
     chunk = min(CHUNK, n_lon // 4)
     span = chunk * BLK
 
-    lon = lax.axis_index("lon")
-    peers = jnp.stack(
-        [
-            lax.rem(lon // (2 * ny) + a, nz) * (2 * ny) + lax.rem(lax.rem(lon // 2, ny) + b, ny) * 2 + lax.rem(lon + c, 2)
-            for a, b, c in order
-        ]
-    )
-    owner = owners[:, 0, :]
-    match = owner[:, None, :] == peers[None, :, None]
-    pick = jnp.sum(jnp.where(match, jnp.arange(blocks, dtype=jnp.int32)[None, None, :], 0), axis=2)
-    slotk = jnp.sum(jnp.where(match, jnp.arange(n_lon, dtype=jnp.int32)[None, :, None], 0), axis=1)
-
-    smem = pl.BlockSpec(memory_space=pltpu.SMEM)
-    hbm = pl.BlockSpec(memory_space=pl.ANY)
+    hbm = pl.BlockSpec(memory_space=pltpu.HBM)
     dma = pltpu.SemaphoreType.DMA
     body = functools.partial(kernel, n_lon, n_lat)
     slots = 2
     field = (rows, fields, width, levels)
     result = pl.pallas_call(
         body,
-        out_shape=jax.ShapeDtypeStruct(field, F32),
-        in_specs=[smem, smem] + [hbm] * 8,
-        out_specs=hbm,
+        out_shape=pltpu.VMEM(field, F32),
+        in_specs=[hbm] * 9,
+        out_specs=pl.BlockSpec(memory_space=pltpu.VMEM),
         scratch_shapes=[
             pltpu.VMEM((rows + 2, fields, width + 2 * PAD, levels), F32),
             pltpu.VMEM((rows + 2, fields, width + 2 * PAD, levels), F32),
-            pltpu.VMEM((rows, width, levels), F32),
+            pltpu.VMEM((rows + 2, width, levels), F32),
             pltpu.VMEM((slots, blocks, BLK, channels), BF16),
             pltpu.VMEM((slots, blocks, BLK, cin), BF16),
             pltpu.VMEM((slots, n_lon, BLK, channels), BF16),
@@ -458,13 +490,17 @@
             pltpu.VMEM((h2, channels), BF16),
             pltpu.VMEM((1, channels), F32),
             pltpu.VMEM(field, F32),
-            pltpu.VMEM(field, F32),
-            pltpu.VMEM(field, F32),
-            pltpu.VMEM((2, rows + 1, fields, width, levels), F32),
-            pltpu.VMEM((2, rows + 1, fields, width, levels), F32),
+            pltpu.VMEM((rows + 2, fields, width, levels), F32),
+            pltpu.VMEM((rows + 2, fields, width, levels), F32),
+            pltpu.VMEM((2, 2, fields, width, levels), BF16),
+            pltpu.VMEM((2, 2, fields, width, levels), BF16),
             pltpu.VMEM((2, fields, width + 2 * PAD, levels), F32),
             pltpu.VMEM((4, 2, rows, 8, levels), F32),
             pltpu.VMEM((4, 2, rows, 8, levels), F32),
+            pltpu.SMEM((slots, 1, blocks), jnp.int32),
+            pltpu.SMEM((slots, n_lon), jnp.int32),
+            pltpu.SMEM((slots, blocks), jnp.int32),
+            pltpu.SMEM((n_lon,), jnp.int32),
             pltpu.VMEM((span, h1), BF16),
             pltpu.VMEM((span, h1), F32),
             pltpu.VMEM((span, h2), BF16),
@@ -472,8 +508,7 @@
             pltpu.VMEM((span, channels), BF16),
             pltpu.VMEM((span, h2), BF16),
             pltpu.VMEM((span, h1), BF16),
-            dma((8,)),
-            dma,
+            dma((10,)),
             dma((slots,)),
             dma((slots, n_lon // chunk)),
             dma((slots,)),
@@ -486,12 +521,11 @@
             dma((4, 2)),
         ],
         compiler_params=pltpu.CompilerParams(
-            collective_id=0, has_side_effects=True, vmem_limit_bytes=56 * 2**20
+            collective_id=0, has_side_effects=True, vmem_limit_bytes=60 * 2**20
         ),
         name="gradient",
     )(
-        pick,
-        slotk,
+        owners,
         state.transpose(0, 2, 1, 3),
         background.transpose(0, 2, 1, 3),
         diffusivity,

time: 116 us -> 113 us (0.974)
  local copies, waits for them, and re-layouts: 2.84 us -> 1.15 us
  other arithmetic: 1.44 us -> 0 us
    unnamed x1, local copies, waits for them, and re-layouts: 2.73 us -> 1.15 us
    reduce_sum x1 -> x0, other arithmetic: 1.44 us -> none  [shards(): jnp.sum(jnp.where(match, jnp.arange(n_lon, dtype=jnp.int32)[None, :, None...]
where the time goes in v1:
time: 113 us; the launch traced here: 112 us
  Pallas kernels  111 us (98%)
  local copies, waits for them, and re-layouts  1.15 us (1%)
    pallas_call x1, Pallas kernels, shards(): pl.pallas_call(body, out_shape=pltpu.VMEM(field, F32), in_specs=[hbm] * 9...  111 us

profile of v1, /device:TPU:0, one launch (start us, length us, event | category | flops | bytes accessed | tf_op | source)
XLA Modules:
  0.0 112.1 jit_solution(3437368224870964829)
XLA Ops:
  0.0 110.9 %gradient.1 = f32[8,6,64,128]{3,2,1,0:T(8,128)S(1)} custom-call(s32[2,1,16]{2,1,0:T(1,128)} %own_h.1, f32[8,6,64,128]{3,2,1,0:T(8,128)} %bitcast.9, f32[8,6,64,128]{3,2,1,0:T(8,128)} %bitcast.10, f32[8,64,128]{2,1,0:T(8,128)} %kd.1, bf16[2,16,32,512]{3,2,1,0:T(8,128)(2,1)} %bitcast.12, bf16[768,1024]{1,0:T(8,128)(2,1)} %bitcast.11, ...), custom_call_target="tpu_custom_call" | custom-call | tf_op jit(solution)/shard_map/gradient/pallas_call | solution.py:470
  110.9 1.1 %copy.11 = f32[8,64,6,128]{3,1,2,0:T(8,128)} copy(f32[8,64,6,128]{3,1,2,0:T(8,128)S(1)} %bitcast.7) | data formatting | bytes 3145728

commit v2 on v1

--- a/solution.py
+++ b/solution.py
@@ -38,7 +38,7 @@
         for e in (d, opposite):
             if e not in chips:
                 chips.append(e)
-    return [(0, 0, 0), (0, 0, 1)] + [(a, b, c) for c in (0, 1) for a, b in chips]
+    return [(0, 0, 0), (0, 0, 1)] + [(a, b, c) for c in (0, 1) for n, (a, b) in enumerate(chips)]
 
 
 def kernel(
@@ -245,12 +245,12 @@
     dispatch(1, send_r, recv_r, rs_sem, rr_sem)
     find_blocks(0)
     pack(0, rst, send_r, recv_r)
-    dispatch(0, send_r, recv_r, rs_sem, rr_sem)
     loads[2].wait()
     take_state(0, s0)
     advance(s0, 0, s1)
     pack_state(1, s1)
     send_state(1, s1)
+    dispatch(0, send_r, recv_r, rs_sem, rr_sem)
     take_state(1, s1)
     advance(s1, 1, None)
     send_columns(1)

time: 113 us -> 109 us (0.965)
  Pallas kernels: 111 us -> 107 us
    pallas_call x1, Pallas kernels: 111 us -> 107 us  [shards(): pl.pallas_call(body, out_shape=pltpu.VMEM(field, F32), in_specs=[hbm] * 9...]
where the time goes in v2:
time: 109 us
  Pallas kernels  107 us (98%)
  local copies, waits for them, and re-layouts  1.15 us (1%)
    pallas_call x1, Pallas kernels, shards(): pl.pallas_call(body, out_shape=pltpu.VMEM(field, F32), in_specs=[hbm] * 9...  107 us

profile of v2, /device:TPU:0, one launch (start us, length us, event | category | flops | bytes accessed | tf_op | source)
XLA Modules:
  0.0 108.5 jit_solution(7666465128170888689)
XLA Ops:
  0.0 107.4 %gradient.1 = f32[8,6,64,128]{3,2,1,0:T(8,128)S(1)} custom-call(s32[2,1,16]{2,1,0:T(1,128)} %own_h.1, f32[8,6,64,128]{3,2,1,0:T(8,128)} %bitcast.9, f32[8,6,64,128]{3,2,1,0:T(8,128)} %bitcast.10, f32[8,64,128]{2,1,0:T(8,128)} %kd.1, bf16[2,16,32,512]{3,2,1,0:T(8,128)(2,1)} %bitcast.12, bf16[768,1024]{1,0:T(8,128)(2,1)} %bitcast.11, ...), custom_call_target="tpu_custom_call" | custom-call | tf_op jit(solution)/shard_map/gradient/pallas_call | solution.py:470
  107.4 1.1 %copy.11 = f32[8,64,6,128]{3,1,2,0:T(8,128)} copy(f32[8,64,6,128]{3,1,2,0:T(8,128)S(1)} %bitcast.7) | data formatting | bytes 3145728

commit v3 on v2

--- a/solution.py
+++ b/solution.py
@@ -14,6 +14,7 @@
 VERTICAL = 0.1
 BLK = 32
 CHUNK = 8
+HELD = 2
 TILE = 256
 PAD = 8
 
@@ -33,7 +34,7 @@
         return min(d[0], nz - d[0]) + min(d[1], ny - d[1])
 
     chips = []
-    for d in sorted(((a, b) for a in range(nz) for b in range(ny) if a or b), key=lambda d: (hops(d), d)):
+    for d in sorted(((a, b) for a in range(nz) for b in range(ny) if a or b), key=lambda d: (0 in d and hops(d) > 1, hops(d), -d[0])):
         opposite = ((nz - d[0]) % nz, (ny - d[1]) % ny)
         for e in (d, opposite):
             if e not in chips:
@@ -292,6 +293,16 @@
                 part = got.at[slot, pl.ds(1, chunk - 1)] if first else got.at[slot, pl.ds(g * chunk, chunk)]
                 pltpu.make_async_copy(part, part, sem.at[slot, g]).wait()
 
+    def reply(home, g):
+        replies = rep_r[home]
+        for k in range(g * chunk, (g + 1) * chunk):
+            if k == 0:
+                replies[0] = rep_s[home, 0]
+            else:
+                remote(
+                    rep_s.at[home, k], replies.at[k], ps_sem.at[home], pr_sem.at[home], back(k)
+                ).start()
+
     @pl.loop(0, 2 * chunks)
     def _(t):
         slot = 1 - t // chunks
@@ -315,18 +326,10 @@
             rep_s[slot, pl.ds(base, chunk), :, n] = (
                 nt(gg1[...], w1[n, :]).astype(BF16).reshape(chunk, BLK, n.stop - n.start)
             )
-        for tt in range(2 * chunks):
+        for tt in range(2 * chunks - HELD):
             @pl.when(t == tt)
             def _():
-                home, replies = 1 - tt // chunks, rep_r[1 - tt // chunks]
-                for k in range(tt % chunks * chunk, (tt % chunks + 1) * chunk):
-                    if k == 0:
-                        replies[0] = rep_s[home, 0]
-                    else:
-                        remote(
-                            rep_s.at[home, k], replies.at[k], ps_sem.at[home],
-                            pr_sem.at[home], back(k),
-                        ).start()
+                reply(1 - tt // chunks, tt % chunks)
 
 
     def wait_replies(slot):
@@ -433,6 +436,8 @@
 
     send_rims(2, s1, frc_a)
     send_sides(2, s1, frc_a)
+    for g in range(chunks - HELD, chunks):
+        reply(0, g)
     transpose_tile(s1, frc_a, frc_b, 1, None)
     add_sides(2, frc_b, 1)
     add_rims(2, frc_b, 1)

time: 109 us -> 108 us (level)
  no operation moved by 1% of the time
where the time goes in v3:
time: 108 us
  Pallas kernels  107 us (99%)
  local copies, waits for them, and re-layouts  1.15 us (1%)
    pallas_call x1, Pallas kernels, shards(): pl.pallas_call(body, out_shape=pltpu.VMEM(field, F32), in_specs=[hbm] * 9...  107 us

profile of v3, /device:TPU:0, one launch (start us, length us, event | category | flops | bytes accessed | tf_op | source)
XLA Modules:
  0.0 108.0 jit_solution(15000913582848856004)
XLA Ops:
  0.0 106.9 %gradient.1 = f32[8,6,64,128]{3,2,1,0:T(8,128)S(1)} custom-call(s32[2,1,16]{2,1,0:T(1,128)} %own_h.1, f32[8,6,64,128]{3,2,1,0:T(8,128)} %bitcast.9, f32[8,6,64,128]{3,2,1,0:T(8,128)} %bitcast.10, f32[8,64,128]{2,1,0:T(8,128)} %kd.1, bf16[2,16,32,512]{3,2,1,0:T(8,128)(2,1)} %bitcast.12, bf16[768,1024]{1,0:T(8,128)(2,1)} %bitcast.11, ...), custom_call_target="tpu_custom_call" | custom-call | tf_op jit(solution)/shard_map/gradient/pallas_call | solution.py:475
  106.9 1.1 %copy.11 = f32[8,64,6,128]{3,1,2,0:T(8,128)} copy(f32[8,64,6,128]{3,1,2,0:T(8,128)S(1)} %bitcast.7) | data formatting | bytes 3145728

commit v4 on v3

--- a/solution.py
+++ b/solution.py
@@ -154,7 +154,7 @@
         )
 
     def pack_state(phase, s):
-        @pl.loop(0, rows)
+        @pl.loop(0, rows, unroll=True)
         def _(i):
             for f in range(fields):
                 edge_s[phase, 0, i, f : f + 1, :] = s[i + 1, f, PAD + width - 1 : PAD + width, :]
@@ -168,7 +168,7 @@
         wait_rows(phase, *state_rows(s))
         wait_edges(phase)
 
-        @pl.loop(0, rows)
+        @pl.loop(0, rows, unroll=True)
         def _(i):
             for f in range(fields):
                 s[i + 1, f, PAD - 1 : PAD, :] = edge_r[phase, 0, i, f : f + 1, :]
@@ -353,7 +353,7 @@
         send_rows(phase, *rims(phase))
 
     def send_sides(phase, s, g):
-        @pl.loop(0, rows)
+        @pl.loop(0, rows, unroll=True)
         def _(i):
             for side, j, sign in ((0, width - 1, -1.0), (1, 0, 1.0)):
                 coef = kap[i + 1, j : j + 1, :] + (sign * ADVECT) * s[i + 1, 0, PAD + j : PAD + j + 1, :]
@@ -407,7 +407,7 @@
     def add_sides(phase, into, shift):
         wait_edges(phase)
 
-        @pl.loop(0, rows)
+        @pl.loop(0, rows, unroll=True)
         def _(i):
             for f in range(fields):
                 into[i + shift, f, 0:1, :] += edge_r[phase, 0, i, f : f + 1, :]

time: 108 us -> 108 us (level)
  no operation moved by 1% of the time
where the time goes in v4:
time: 108 us
  Pallas kernels  107 us (99%)
  local copies, waits for them, and re-layouts  1.15 us (1%)
    pallas_call x1, Pallas kernels, shards(): pl.pallas_call(body, out_shape=pltpu.VMEM(field, F32), in_specs=[hbm] * 9...  107 us

profile of v4, /device:TPU:0, one launch (start us, length us, event | category | flops | bytes accessed | tf_op | source)
XLA Modules:
  0.0 108.0 jit_solution(4266283105364174431)
XLA Ops:
  0.0 106.9 %gradient.1 = f32[8,6,64,128]{3,2,1,0:T(8,128)S(1)} custom-call(s32[2,1,16]{2,1,0:T(1,128)} %own_h.1, f32[8,6,64,128]{3,2,1,0:T(8,128)} %bitcast.9, f32[8,6,64,128]{3,2,1,0:T(8,128)} %bitcast.10, f32[8,64,128]{2,1,0:T(8,128)} %kd.1, bf16[2,16,32,512]{3,2,1,0:T(8,128)(2,1)} %bitcast.12, bf16[768,1024]{1,0:T(8,128)(2,1)} %bitcast.11, ...), custom_call_target="tpu_custom_call" | custom-call | tf_op jit(solution)/shard_map/gradient/pallas_call | solution.py:475
  106.9 1.1 %copy.11 = f32[8,64,6,128]{3,1,2,0:T(8,128)} copy(f32[8,64,6,128]{3,1,2,0:T(8,128)S(1)} %bitcast.7) | data formatting | bytes 3145728
